TPU v7x, 32 devices: a whole 2x2x4 slice. The times are simulated.
32 devices in a mesh: dp: 16 (over z, y, x), chan: 2 (over core).
Axes of the slice: x: 2, y: 2, z: 4, core: 2. Of those that a mesh axis runs over, the one named last changes fastest.
Arguments:
- frames_in: bfloat16 [2, 16, 1024, 512], P(None, 'dp', None, 'chan'), may hold values from -6 to 6
- utter_lengths: int32 [2, 16, 4], P(None, 'dp'), may hold values from 1 to 64, 128 in all within a row
- code_ids: int32 [2, 16, 128], P(None, 'dp'), may hold values from 0 to 8191
- alpha_first: float32 [3, 512], P(None, 'chan'), may hold values from 0.3 to 2
- alpha_second: float32 [3, 512], P(None, 'chan'), may hold values from 0.3 to 2
- alpha_last: float32 [512], P('chan'), may hold values from 0.3 to 2
- w_dilated: bfloat16 [3, 7, 512, 512], P(None, None, None, 'chan'), may hold values from -0.09375 to 0.09375
- w_point: bfloat16 [3, 512, 512], P(None, None, 'chan'), may hold values from -0.25 to 0.25
- w_down: bfloat16 [16, 512, 1024], P(None, None, 'chan'), may hold values from -0.0625 to 0.0625
- w_latent: bfloat16 [1024, 8], P('chan'), may hold values from -0.0390625 to 0.0390625
- w_expand: bfloat16 [8, 1024], P(None, 'chan'), may hold values from -3 to 3
- codebook: float32 [8, 8192], replicated, may hold values from -6 to 6
- out_grad: bfloat16 [2, 16, 128, 1024], P(None, 'dp', None, 'chan'), may hold values from -6 to 6
Outputs:
- block_out: bfloat16 [2, 16, 128, 1024], P(None, 'dp', None, 'chan')
- grad_frames: float32 [2, 16, 1024, 512], P(None, 'dp', None, 'chan')
- grad_alpha_first: float32 [3, 512], P(None, 'chan')
- grad_alpha_second: float32 [3, 512], P(None, 'chan')
- grad_alpha_last: float32 [512], P('chan')
- grad_w_dilated: float32 [3, 7, 512, 512], P(None, None, None, 'chan')
- grad_w_point: float32 [3, 512, 512], P(None, None, 'chan')
- grad_w_down: float32 [16, 512, 1024], P(None, None, 'chan')
- grad_w_latent: float32 [1024, 8], P('chan')
- grad_w_expand: float32 [8, 1024], P(None, 'chan')
- grad_codebook: float32 [8, 8192], replicated
Inputs may be any that keep to these rules, and one draw needn't show every extreme that they name: `utter_lengths`: each row's 4 utterance lengths count output frames and sum to 128; the longest of each row has exactly 64.
All inputs are finite; a program needn't handle non-finite values.
Results may differ from a plain program's by a relative error of at most 0.035.
Values may be sent and summed in bfloat16 or wider, within the bound.
No kernel may reach another device: no remote copies, remote signals or barrier semaphores. Data moves between devices by JAX's collectives and lax.ppermute only.
A program may use at most 256 MiB of HBM per device.

v0:
```python
import jax
import jax.numpy as jnp
from jax import lax
from jax.sharding import PartitionSpec as P

K = 7
STRIDE = 8
KS = 16


DILATIONS = (1, 3, 9)
HIGHEST_PRECISION = lax.Precision.HIGHEST


def shift_rows(signal, offset):
    if offset > 0:
        zero_rows = jnp.zeros((offset,) + signal.shape[1:], signal.dtype)
        return jnp.concatenate([signal[offset:], zero_rows], axis=0)
    if offset < 0:
        zero_rows = jnp.zeros((-offset,) + signal.shape[1:], signal.dtype)
        return jnp.concatenate([zero_rows, signal[:offset]], axis=0)
    return signal


def utterance_ids(lengths, frames):
    utt_ends = jnp.cumsum(lengths) * STRIDE
    places = jnp.arange(frames, dtype=jnp.int32)
    return 1 + jnp.sum((places[:, None] >= utt_ends[None, :]).astype(jnp.int32), axis=1)


def dilated_taps(signal, labels, dilation):
    pieces = []
    for tap_index in range(K):
        offset = dilation * (tap_index - K // 2)
        same_utt = (shift_rows(labels, offset) == labels).astype(signal.dtype)
        pieces.append(shift_rows(signal, offset) * same_utt[:, None])
    return jnp.concatenate(pieces, axis=1)


def stride_taps(signal, labels):
    frames, channels = signal.shape
    blocks = signal.reshape(frames // STRIDE, STRIDE, channels)
    block_marks = labels[::STRIDE]
    same_before = (shift_rows(block_marks, -1) == block_marks).astype(signal.dtype)
    same_following = (shift_rows(block_marks, 1) == block_marks).astype(signal.dtype)
    before = shift_rows(blocks, -1)[:, STRIDE // 2 :] * same_before[:, None, None]
    following = shift_rows(blocks, 1)[:, : STRIDE // 2] * same_following[:, None, None]
    window = jnp.concatenate([before, blocks, following], axis=1)
    return window.reshape(frames // STRIDE, KS * channels)


def snake_act(signal, sharpness):
    return signal + jnp.square(jnp.sin(sharpness * signal)) / sharpness


def normalize(values, reduce_axis):
    return values * lax.rsqrt(jnp.sum(values * values, axis=reduce_axis, keepdims=True) + 1.0)


def contract_rows(left, right):
    return lax.dot_general(
        left, right, (((0,), (0,)), ((), ())), preferred_element_type=jnp.float32
    )


def contract_cols(left, right):
    return lax.dot_general(
        left, right, (((1,), (1,)), ((), ())), preferred_element_type=jnp.float32
    )


def gather_channels(shard_part):
    return lax.all_gather(shard_part, "chan", axis=1, tiled=True)


def reduce_channels(partial_sum):
    return lax.psum_scatter(
        partial_sum.astype(jnp.bfloat16), "chan", scatter_dimension=1, tiled=True
    ).astype(jnp.float32)


def shards(
    frames_in,
    utter_lengths,
    code_ids,
    alpha_first,
    alpha_second,
    alpha_last,
    w_dilated,
    w_point,
    w_down,
    w_latent,
    w_expand,
    codebook,
    out_grad,
):
    batches = frames_in.shape[0]
    frames = frames_in.shape[2]
    narrow_width = frames_in.shape[3]
    full_width = w_dilated.shape[2]
    out_width = w_down.shape[2]
    latent_width = codebook.shape[0]
    dilated_flat = w_dilated.reshape(3, K * full_width, narrow_width)
    down_flat = w_down.reshape(KS * full_width, out_width)
    latent_wide = w_latent.astype(jnp.float32)
    code_unit, code_back = jax.vjp(lambda values: normalize(values, 0), codebook)
    code_range = jnp.arange(codebook.shape[1], dtype=jnp.int32)
    taps_zeros = jnp.zeros((frames, full_width), jnp.float32)
    channel_zeros = jnp.zeros((narrow_width,), jnp.float32)
    first_sums = [channel_zeros, channel_zeros, channel_zeros]
    second_sums = [channel_zeros, channel_zeros, channel_zeros]
    last_sum = channel_zeros
    dilated_zero = jnp.zeros((K * full_width, narrow_width), jnp.float32)
    dilated_sums = [dilated_zero, dilated_zero, dilated_zero]
    point_zero = jnp.zeros((full_width, narrow_width), jnp.float32)
    point_sums = [point_zero, point_zero, point_zero]
    down_sum = jnp.zeros((KS * full_width, out_width), jnp.float32)
    latent_sum = jnp.zeros((out_width, latent_width), jnp.float32)
    expand_sum = jnp.zeros((latent_width, out_width), jnp.float32)
    code_sum = jnp.zeros(codebook.shape, jnp.float32)
    outputs = []
    input_grads = []
    for batch_index in range(batches):
        signal = frames_in[batch_index, 0].astype(jnp.float32)
        labels = utterance_ids(utter_lengths[batch_index, 0], frames)
        selector = (code_ids[batch_index, 0][:, None] == code_range[None, :]).astype(jnp.float32)
        running = signal
        stored = []
        for section_index in range(3):
            opened = snake_act(running, alpha_first[section_index]).astype(jnp.bfloat16)
            opened_all = gather_channels(opened)
            stacked = dilated_taps(opened_all, labels, DILATIONS[section_index])
            dilated_out = jnp.dot(
                stacked, dilated_flat[section_index], preferred_element_type=jnp.float32
            )
            closed = snake_act(dilated_out, alpha_second[section_index]).astype(jnp.bfloat16)
            closed_all = gather_channels(closed)
            stored.append((running, opened, opened_all, dilated_out, closed, closed_all))
            running = running + jnp.dot(
                closed_all, w_point[section_index], preferred_element_type=jnp.float32
            )
        opened_last = snake_act(running, alpha_last).astype(jnp.bfloat16)
        last_all = gather_channels(opened_last)
        window = stride_taps(last_all, labels)
        hidden = jnp.dot(window, down_flat, preferred_element_type=jnp.float32).astype(jnp.bfloat16)
        latent = lax.psum(jnp.dot(hidden, w_latent, preferred_element_type=jnp.float32), "chan")
        latent_unit, latent_back = jax.vjp(lambda values: normalize(values, 1), latent)
        chosen = lax.dot_general(
            selector,
            code_unit,
            (((1,), (1,)), ((), ())),
            precision=HIGHEST_PRECISION,
            preferred_element_type=jnp.float32,
        )
        mixed_code = (latent_unit + chosen).astype(jnp.bfloat16)
        outputs.append(
            jnp.dot(mixed_code, w_expand, preferred_element_type=jnp.float32).astype(jnp.bfloat16)
        )
        grad_block = out_grad[batch_index, 0]
        expand_sum = expand_sum + contract_rows(mixed_code, grad_block)
        grad_mixed = lax.psum(contract_cols(grad_block, w_expand), "chan")
        code_sum = code_sum + lax.dot_general(
            grad_mixed,
            selector,
            (((0,), (0,)), ((), ())),
            precision=HIGHEST_PRECISION,
            preferred_element_type=jnp.float32,
        )
        grad_latent = latent_back(grad_mixed)[0]
        latent_sum = latent_sum + lax.dot_general(
            hidden.astype(jnp.float32),
            grad_latent,
            (((0,), (0,)), ((), ())),
            precision=HIGHEST_PRECISION,
            preferred_element_type=jnp.float32,
        )
        grad_hidden = lax.dot_general(
            grad_latent,
            latent_wide,
            (((1,), (1,)), ((), ())),
            precision=HIGHEST_PRECISION,
            preferred_element_type=jnp.float32,
        ).astype(jnp.bfloat16)
        down_sum = down_sum + contract_rows(window, grad_hidden)
        grad_window = contract_cols(grad_hidden, down_flat)
        grad_last_all = jax.vjp(lambda values: stride_taps(values, labels), taps_zeros)[1](
            grad_window
        )[0]
        grad_last = reduce_channels(grad_last_all)
        grad_running, grad_rate = jax.vjp(snake_act, running, alpha_last)[1](grad_last)
        last_sum = last_sum + grad_rate
        if batch_index == batches - 1:
            finished = (last_sum, down_sum, latent_sum, expand_sum, code_sum)
        for section_index in (2, 1, 0):
            running_in, opened, kept_opened, dilated_out, closed, kept_closed = stored[
                section_index
            ]
            opened_all = kept_opened
            closed_all = kept_closed
            grad_point = grad_running.astype(jnp.bfloat16)
            point_sums[section_index] = point_sums[section_index] + contract_rows(
                closed_all, grad_point
            )
            grad_closed = reduce_channels(contract_cols(grad_point, w_point[section_index]))
            grad_dilated, grad_rate = jax.vjp(snake_act, dilated_out, alpha_second[section_index])[
                1
            ](grad_closed)
            second_sums[section_index] = second_sums[section_index] + grad_rate
            grad_dilated = grad_dilated.astype(jnp.bfloat16)
            stacked = dilated_taps(opened_all, labels, DILATIONS[section_index])
            dilated_sums[section_index] = dilated_sums[section_index] + contract_rows(
                stacked, grad_dilated
            )
            grad_stacked = contract_cols(grad_dilated, dilated_flat[section_index])
            grad_opened_all = jax.vjp(
                lambda values: dilated_taps(values, labels, DILATIONS[section_index]), taps_zeros
            )[1](grad_stacked)[0]
            grad_opened = reduce_channels(grad_opened_all)
            grad_input, grad_rate = jax.vjp(snake_act, running_in, alpha_first[section_index])[1](
                grad_opened
            )
            first_sums[section_index] = first_sums[section_index] + grad_rate
            grad_running = grad_running + grad_input
        input_grads.append(grad_running)
    (
        first_total,
        second_total,
        dilated_total,
        point_total,
        last_total,
        down_total,
        latent_total,
        expand_total,
        code_total,
    ) = lax.psum(
        (
            jnp.stack(first_sums),
            jnp.stack(second_sums),
            jnp.stack(dilated_sums),
            jnp.stack(point_sums),
            finished[0],
            finished[1],
            finished[2],
            finished[3],
            finished[4],
        ),
        "dp",
    )
    grad_codebook = code_back(code_total)[0]
    block_out = jnp.stack(outputs)[:, None]
    grad_frames = jnp.stack(input_grads)[:, None]
    return (
        block_out,
        grad_frames,
        first_total,
        second_total,
        last_total,
        dilated_total.reshape(3, K, full_width, narrow_width),
        point_total,
        down_total.reshape(KS, full_width, out_width),
        latent_total,
        expand_total,
        grad_codebook,
    )


def solution(mesh):
    placed = (
        P(None, "dp", None, "chan"),
        P(None, "dp", None),
        P(None, "dp", None),
        P(None, "chan"),
        P(None, "chan"),
        P("chan"),
        P(None, None, None, "chan"),
        P(None, None, "chan"),
        P(None, None, "chan"),
        P("chan", None),
        P(None, "chan"),
        P(),
        P(None, "dp", None, "chan"),
    )
    return jax.shard_map(
        shards,
        mesh=mesh,
        in_specs=placed,
        out_specs=(
            P(None, "dp", None, "chan"),
            P(None, "dp", None, "chan"),
            P(None, "chan"),
            P(None, "chan"),
            P("chan"),
            P(None, None, None, "chan"),
            P(None, None, "chan"),
            P(None, None, "chan"),
            P("chan", None),
            P(None, "chan"),
            P(),
        ),
        check_vma=False,
    )
```

profile of v0, /device:TPU:0, one launch (start us, length us, event | category | flops | bytes accessed | tf_op | source)
XLA Modules:
  0.0 1546.3 jit_solution(5749000743729496618)
XLA Ops:
  9.2 8.8 fusion.131
  47.7 10.9 add_convert_fusion.5
  59.4 9.6 all-gather.17.cloned.1.call-done
  70.9 10.3 all-gather.31.cloned.1.call-done
  81.2 9.4 add_convert_fusion.4
  91.2 9.7 all-gather.19.cloned.1.call-done
  118.3 10.8 add_convert_fusion.3
  130.2 9.3 all-gather.21.cloned.1.call-done
  141.2 10.6 all-gather.35.cloned.1.call-done
  151.9 9.2 add_convert_fusion.2
  161.8 9.7 all-gather.23.cloned.1.call-done
  188.2 10.9 add_convert_fusion.1
  200.2 9.3 all-gather.25.cloned.1.call-done
  211.5 10.1 all-gather.39.cloned.1.call-done
  221.7 9.3 add_convert_fusion
  232.1 9.2 all-gather.27.cloned.1.call-done
  288.1 12.5 reduce-scatter.29.cloned.1.call-done
  300.6 10.7 fusion.70
  324.3 10.1 fusion.220
  334.4 9.0 fusion.267
  354.1 10.1 fusion.208
  364.3 8.9 fusion.266
  400.3 8.5 fusion.309
  408.8 18.5 %fusion.80 = (f32[256]{0:T(256)}, f32[256]{0:T(256)}, f32[256]{0:T(256)}, f32[256]{0:T(256)}, f32[1024,256]{1,0:T(8,128)S(1)}, /*index=5*/f32[1024,256]{1,0:T(8,128)S(1)}) fusion(bf16[1024,256]{1,0:T(8,128)(2,1)} %reduce-scatter.19.cloned.1.call-done, f32[1024,256]{1,0:T(8,128)} %copy-done.12, f32[256]{0:T(256)S(1)} %bitcast.304, f32[256]{0:T(256)S(1)} %bitcast.306, ...), kind=kLoop, calls=%fused_computation.211 | loop fusion | flops 12057600 | bytes 8395776 | tf_op jit(solution)/shard_map/transpose(jvp())/reduce_sum | solution.py:53
  432.3 15.4 convolution_add_fusion
  453.2 10.0 fusion.216
  463.2 8.8 fusion.265
  484.2 10.0 fusion.205
  494.3 8.8 fusion.264
  515.6 8.6 fusion.218
  524.2 10.5 fusion
  537.2 9.9 fusion.90
  549.7 8.6 fusion.214
  558.3 10.4 fusion.1
  575.8 10.0 fusion.212
  585.8 8.9 fusion.262
  606.9 10.1 fusion.202
  617.0 8.9 fusion.263
  638.3 8.6 fusion.210
  646.9 10.6 fusion.2
  666.6 10.0 fusion.75
  676.8 8.3 fusion.85
  685.2 8.3 fusion.95
  693.7 9.4 fusion.62
  704.7 730.5 %all-reduce.113.cloned.1.call-done = (f32[8,8192]{1,0:T(8,128)}, f32[3,7,512,256]{3,2,1,0:T(8,128)}, f32[3,512,256]{2,1,0:T(8,128)}, f32[16,512,512]{2,1,0:T(8,128)}) async-done(((f32[8,8192]{1,0:T(8,128)}, f32[3,7,512,256]{3,2,1,0:T(8,128)}, f32[3,512,256]{2,1,0:T(8,128)}, f32[16,512,512]{2,1,0:T(8,128)}), (f32[8,8192]{1,0:T(8,128)}, f32[3,7,512,256]{3,2,1,0:T(8,128)}, f32[3,512,256]{2,1,0:T(8,128)}, ...) | async-done | bytes 29622288 | tf_op jit(solution)/shard_map/psum | solution.py:235
  1442.8 74.2 %all-reduce.108 = (f32[3,256]{1,0:T(4,128)}, f32[3,256]{1,0:T(4,128)}, f32[256]{0:T(256)}, f32[512,8]{0,1:T(8,128)}, f32[8,512]{1,0:T(8,128)}) all-reduce(f32[3,256]{1,0:T(4,128)S(1)} %pad_maximum_fusion.4, f32[3,256]{1,0:T(4,128)S(1)} %pad_maximum_fusion.5, f32[256]{0:T(256)S(1)} %add_add_fusion.3, ...), channel_id=1, replica_groups=mesh['dp'=16,'chan'=2] {'dp'}, use_global_device_ids=true, to_apply=%region_39.40 | all-reduce | flops 9984 | bytes 79872 | tf_op jit(solution)/shard_map/psum | solution.py:235
  1517.0 9.6 copy.102
  1527.8 11.8 copy.104
  (694 shorter events, 263.3 us)
Async XLA Ops:
  7.2 255.6 %copy-start = (bf16[512,8]{0,1:T(8,128)(2,1)S(1)}, bf16[512,8]{0,1:T(8,128)(2,1)}, u32[]{:S(2)}) copy-start(bf16[512,8]{0,1:T(8,128)(2,1)} %param.22) | copy-start | bytes 24580
  7.2 22.8 %all-gather.15.cloned.1.call-start = ((), (), s32[]{:S(2)}) async-start(), calls=%async_computation.14 | async-start | bytes 1572864 | tf_op jit(solution)/shard_map/all_gather | solution.py:73
  8.7 72.5 %copy-start.162 = (f32[1,256]{1,0:T(1,128)}, f32[1,256]{1,0:T(1,128)S(1)}, u32[]{:S(2)}) copy-start(f32[1,256]{1,0:T(1,128)S(1)} %get-tuple-element.275) | copy-start | bytes 3076
  18.1 24.3 %all-gather.29.cloned.1.call-start = ((), (), s32[]{:S(2)}) async-start(), calls=%async_computation.21 | async-start | bytes 1572864 | tf_op jit(solution)/shard_map/all_gather | solution.py:73
  18.8 50.1 %all-gather.17.cloned.1.call-start = ((), (), s32[]{:S(2)}) async-start(), calls=%async_computation.15 | async-start | bytes 1572864 | tf_op jit(solution)/shard_map/all_gather | solution.py:73
  21.1 26.6 %copy-start.100 = (f32[1,256]{1,0:T(1,128)}, f32[1,256]{1,0:T(1,128)S(1)}, u32[]{:S(2)}) copy-start(f32[1,256]{1,0:T(1,128)S(1)} %get-tuple-element.267) | copy-start | bytes 3076
  21.1 96.7 %copy-start.102 = (f32[1,256]{1,0:T(1,128)}, f32[1,256]{1,0:T(1,128)S(1)}, u32[]{:S(2)}) copy-start(f32[1,256]{1,0:T(1,128)S(1)} %get-tuple-element.269) | copy-start | bytes 3076
  26.7 20.9 %copy-start.9 = (bf16[1,7,512,256]{3,2,1,0:T(8,128)(2,1)}, bf16[1,7,512,256]{3,2,1,0:T(8,128)(2,1)S(1)}, u32[]{:S(2)}) copy-start(bf16[1,7,512,256]{3,2,1,0:T(8,128)(2,1)S(1)} %get-tuple-element.206) | copy-start | bytes 5505028
  58.5 22.6 %copy-start.39 = (bf16[2,1,1024,256]{3,2,1,0:T(8,128)(2,1)S(1)}, bf16[2,1,1024,256]{3,2,1,0:T(8,128)(2,1)}, u32[]{:S(2)}) copy-start(bf16[2,1,1024,256]{3,2,1,0:T(8,128)(2,1)} %param.13) | copy-start | bytes 3145732
  58.6 22.6 %all-gather.31.cloned.1.call-start = ((), (), s32[]{:S(2)}) async-start(), calls=%async_computation.22 | async-start | bytes 1572864 | tf_op jit(solution)/shard_map/all_gather | solution.py:73
  59.1 41.8 %all-gather.19.cloned.1.call-start = ((), (), s32[]{:S(2)}) async-start(), calls=%async_computation.16 | async-start | bytes 1572864 | tf_op jit(solution)/shard_map/all_gather | solution.py:73
  70.8 68.7 %copy-start.13 = (f32[1024,256]{1,0:T(8,128)}, f32[1024,256]{1,0:T(8,128)S(1)}, u32[]{:S(2)}) copy-start(f32[1024,256]{1,0:T(8,128)S(1)} %convert_add_fusion.2) | copy-start | bytes 3145732
  90.6 22.5 %all-gather.33.cloned.1.call-start = ((), (), s32[]{:S(2)}) async-start(), calls=%async_computation.23 | async-start | bytes 1572864 | tf_op jit(solution)/shard_map/all_gather | solution.py:73
  91.2 48.3 %all-gather.21.cloned.1.call-start = ((), (), s32[]{:S(2)}) async-start(), calls=%async_computation.17 | async-start | bytes 1572864 | tf_op jit(solution)/shard_map/all_gather | solution.py:73
  129.2 22.7 %all-gather.35.cloned.1.call-start = ((), (), s32[]{:S(2)}) async-start(), calls=%async_computation.24 | async-start | bytes 1572864 | tf_op jit(solution)/shard_map/all_gather | solution.py:73
  129.9 41.6 %all-gather.23.cloned.1.call-start = ((), (), s32[]{:S(2)}) async-start(), calls=%async_computation.18 | async-start | bytes 1572864 | tf_op jit(solution)/shard_map/all_gather | solution.py:73
  141.2 19.9 %copy-start.12 = (f32[1024,256]{1,0:T(8,128)}, f32[1024,256]{1,0:T(8,128)S(1)}, u32[]{:S(2)}) copy-start(f32[1024,256]{1,0:T(8,128)S(1)} %convolution_add_fusion.8) | copy-start | bytes 3145732
  161.1 22.5 %all-gather.37.cloned.1.call-start = ((), (), s32[]{:S(2)}) async-start(), calls=%async_computation.25 | async-start | bytes 1572864 | tf_op jit(solution)/shard_map/all_gather | solution.py:73
  161.7 47.7 %all-gather.25.cloned.1.call-start = ((), (), s32[]{:S(2)}) async-start(), calls=%async_computation.19 | async-start | bytes 1572864 | tf_op jit(solution)/shard_map/all_gather | solution.py:73
  199.1 22.5 %copy-start.139 = (f32[256]{0:T(256)S(1)}, f32[256]{0:T(256)}, u32[]{:S(2)}) copy-start(f32[256]{0:T(256)} %param.18) | copy-start | bytes 3076
  199.1 22.5 %all-gather.39.cloned.1.call-start = ((), (), s32[]{:S(2)}) async-start(), calls=%async_computation.26 | async-start | bytes 1572864 | tf_op jit(solution)/shard_map/all_gather | solution.py:73
  199.7 41.6 %all-gather.27.cloned.1.call-start = ((), (), s32[]{:S(2)}) async-start(), calls=%async_computation.20 | async-start | bytes 1572864 | tf_op jit(solution)/shard_map/all_gather | solution.py:73
  231.0 22.0 %all-gather.41.cloned.1.call-start = ((), (), s32[]{:S(2)}) async-start(), calls=%async_computation.27 | async-start | bytes 1572864 | tf_op jit(solution)/shard_map/all_gather | solution.py:73
  231.6 56.6 %reduce-scatter.15.cloned.1.call-start = ((), (), s32[]{:S(2)}) async-start(), calls=%async_computation.28 | async-start | bytes 1572864 | tf_op jit(solution)/shard_map/reduce_scatter | solution.py:77
  268.4 129.8 %copy-start.114 = (f32[128,8]{0,1:T(8,128)}, f32[128,8]{0,1:T(8,128)S(1)}, u32[]{:S(2)}) copy-start(f32[128,8]{0,1:T(8,128)S(1)} %get-tuple-element.101) | copy-start | bytes 12292
  268.4 161.7 %copy-start.112 = (f32[128,8]{0,1:T(8,128)}, f32[128,8]{0,1:T(8,128)S(1)}, u32[]{:S(2)}) copy-start(f32[128,8]{0,1:T(8,128)S(1)} %get-tuple-element.102) | copy-start | bytes 12292
  278.2 22.4 %reduce-scatter.29.cloned.1.call-start = ((), (), s32[]{:S(2)}) async-start(), calls=%async_computation.35 | async-start | bytes 1572864 | tf_op jit(solution)/shard_map/reduce_scatter | solution.py:77
  288.0 36.3 %reduce-scatter.17.cloned.1.call-start = ((), (), s32[]{:S(2)}) async-start(), calls=%async_computation.29 | async-start | bytes 1572864 | tf_op jit(solution)/shard_map/reduce_scatter | solution.py:77
  314.5 39.7 %reduce-scatter.31.cloned.1.call-start = ((), (), s32[]{:S(2)}) async-start(), calls=%async_computation.36 | async-start | bytes 1572864 | tf_op jit(solution)/shard_map/reduce_scatter | solution.py:77
  317.5 91.3 %reduce-scatter.19.cloned.1.call-start = ((), (), s32[]{:S(2)}) async-start(), calls=%async_computation.30 | async-start | bytes 1572864 | tf_op jit(solution)/shard_map/reduce_scatter | solution.py:77
  353.8 55.0 %reduce-scatter.33.cloned.1.call-start = ((), (), s32[]{:S(2)}) async-start(), calls=%async_computation.37 | async-start | bytes 1572864 | tf_op jit(solution)/shard_map/reduce_scatter | solution.py:77
  382.9 70.2 %reduce-scatter.21.cloned.1.call-start = ((), (), s32[]{:S(2)}) async-start(), calls=%async_computation.31 | async-start | bytes 1572864 | tf_op jit(solution)/shard_map/reduce_scatter | solution.py:77
  385.3 44.8 %copy-start.169 = (s32[128]{0:T(128)}, s32[128]{0:T(128)S(1)}, u32[]{:S(2)}) copy-start(s32[128]{0:T(128)S(1)} %get-tuple-element.357) | copy-start | bytes 1540
  427.4 107.3 %copy-start.8 = (f32[1024,256]{1,0:T(8,128)}, f32[1024,256]{1,0:T(8,128)S(1)}, u32[]{:S(2)}) copy-start(f32[1024,256]{1,0:T(8,128)S(1)} %get-tuple-element.219) | copy-start | bytes 3145732
  430.0 54.2 %reduce-scatter.35.cloned.1.call-start = ((), (), s32[]{:S(2)}) async-start(), calls=%async_computation.38 | async-start | bytes 1572864 | tf_op jit(solution)/shard_map/reduce_scatter | solution.py:77
  432.3 15.4 copy-start.84
  452.9 84.3 %reduce-scatter.23.cloned.1.call-start = ((), (), s32[]{:S(2)}) async-start(), calls=%async_computation.32 | async-start | bytes 1572864 | tf_op jit(solution)/shard_map/reduce_scatter | solution.py:77
  484.2 53.1 %reduce-scatter.37.cloned.1.call-start = ((), (), s32[]{:S(2)}) async-start(), calls=%async_computation.39 | async-start | bytes 1572864 | tf_op jit(solution)/shard_map/reduce_scatter | solution.py:77
  515.1 60.2 %reduce-scatter.25.cloned.1.call-start = ((), (), s32[]{:S(2)}) async-start(), calls=%async_computation.33 | async-start | bytes 1572864 | tf_op jit(solution)/shard_map/reduce_scatter | solution.py:77
  549.6 57.3 %reduce-scatter.39.cloned.1.call-start = ((), (), s32[]{:S(2)}) async-start(), calls=%async_computation.40 | async-start | bytes 1572864 | tf_op jit(solution)/shard_map/reduce_scatter | solution.py:77
  571.2 122.4 %reduce-scatter.27.cloned.1.call-start = ((), (), s32[]{:S(2)}) async-start(), calls=%async_computation.34 | async-start | bytes 1572864 | tf_op jit(solution)/shard_map/reduce_scatter | solution.py:77
  606.8 86.8 %reduce-scatter.41.cloned.1.call-start = ((), (), s32[]{:S(2)}) async-start(), calls=%async_computation.41 | async-start | bytes 1572864 | tf_op jit(solution)/shard_map/reduce_scatter | solution.py:77
  638.1 797.1 %all-reduce.113.cloned.1.call-start = ((), (), s32[]{:S(2)}) async-start(), calls=%async_computation.42 | async-start | bytes 59244544 | tf_op jit(solution)/shard_map/psum | solution.py:235
  703.2 732.0 %copy-start.86 = (f32[8,8192]{1,0:T(8,128)S(1)}, f32[8,8192]{1,0:T(8,128)}, u32[]{:S(2)}) copy-start(f32[8,8192]{1,0:T(8,128)} %param.24) | copy-start | bytes 786436
  703.2 733.2 %copy-start.170 = (s32[128]{0:T(128)S(1)}, s32[128]{0:T(128)}, u32[]{:S(2)}) copy-start(s32[128]{0:T(128)} %copy-done.169) | copy-start | bytes 1540
  703.2 735.3 %copy-start.168 = (s32[128]{0:T(128)S(1)}, s32[128]{0:T(128)}, u32[]{:S(2)}) copy-start(s32[128]{0:T(128)} %copy-done.167) | copy-start | bytes 1540
  704.7 735.9 %copy-start.117 = (bf16[8,512]{1,0:T(8,128)(2,1)S(1)}, bf16[8,512]{1,0:T(8,128)(2,1)}, u32[]{:S(2)}) copy-start(bf16[8,512]{1,0:T(8,128)(2,1)} %param.23) | copy-start | bytes 24580
  704.7 736.2 %copy-start.93 = (bf16[2,1,128,512]{3,2,1,0:T(8,128)(2,1)S(1)}, bf16[2,1,128,512]{3,2,1,0:T(8,128)(2,1)}, u32[]{:S(2)}) copy-start(bf16[2,1,128,512]{3,2,1,0:T(8,128)(2,1)} %param.25) | copy-start | bytes 786436
  (155 other events, 704.8 us)
Sparse Core Ops, SparseCore 0:
  18.2 11.7 all-gather.14
  32.1 10.1 all-gather.28
  58.7 10.2 all-gather.16
  70.9 10.1 all-gather.30
  90.7 10.1 all-gather.18
  102.9 10.1 all-gather.32
  129.3 10.1 all-gather.20
  141.6 10.1 all-gather.34
  161.3 10.1 all-gather.22
  173.5 10.1 all-gather.36
  199.3 10.1 all-gather.24
  211.4 10.1 all-gather.38
  231.1 10.1 all-gather.26
  242.7 10.1 all-gather.40
  278.3 9.8 reduce-scatter.14
  290.9 9.6 reduce-scatter.28
  314.6 9.6 reduce-scatter.16
  326.5 9.6 reduce-scatter.30
  353.9 9.6 reduce-scatter.18
  383.1 9.7 reduce-scatter.32
  430.1 9.8 reduce-scatter.20
  453.0 9.8 reduce-scatter.34
  484.3 9.8 reduce-scatter.22
  515.2 9.8 reduce-scatter.36
  549.7 9.7 reduce-scatter.24
  571.3 9.7 reduce-scatter.38
  607.0 9.7 reduce-scatter.26
  638.2 9.7 reduce-scatter.40
  665.5 769.6 all-reduce.112
where the time goes:
time: 1560 us; the launch traced here: 1550 us
  waiting for transfers between devices  856 us (55%)
  matrix products  264 us (17%)
  other arithmetic  167 us (11%)
  local copies, waits for them, and re-layouts  161 us (10%)
  blocking collectives  77.7 us (5%)
  between operations  17.3 us (1%)
    psum x1, waiting for transfers between devices, shards(): lax.psum((jnp.stack(first_sums), jnp.stack(second_sums), jnp.stack(dilate...  731 us
    all_gather x14, waiting for transfers between devices, gather_channels(): return lax.all_gather(shard_part, 'chan', axis=1, tiled=True)  103 us
    dot_general x16, matrix products, contract_cols(): lax.dot_general(left, right, (((1,), (1,)), ((), ())), preferred_element_...  88.2 us
    dot_general x16, matrix products, contract_rows(): lax.dot_general(left, right, (((0,), (0,)), ((), ())), preferred_element_...  85.7 us
    reduce_sum x7, other arithmetic, snake_act(): return signal + jnp.square(jnp.sin(sharpness * signal)) / sharpness  75.2 us
    psum x1, blocking collectives, shards(): lax.psum((jnp.stack(first_sums), jnp.stack(second_sums), jnp.stack(dilate...  74.2 us
    unnamed x357, local copies, waits for them, and re-layouts  64.7 us
    split x6, local copies, waits for them, and re-layouts, dilated_taps(): return jnp.concatenate(pieces, axis=1)  53.3 us
  transfers between devices with their start and end apart: 29, of which 18 were waited for; matrix products, arithmetic and copies ran while one was open for 24% of the time, Pallas kernels for 0%

commit v1 on v0

v1 whole, which is shorter than its diff:
```python
import jax
import jax.numpy as jnp
from jax import lax
from jax.sharding import PartitionSpec as P

K = 7
STRIDE = 8
KS = 16
DILATIONS = (1, 3, 9)
HIGHEST = lax.Precision.HIGHEST
BF = jnp.bfloat16
F32 = jnp.float32


def shift_rows(signal, offset):
    if offset > 0:
        zero_rows = jnp.zeros((offset,) + signal.shape[1:], signal.dtype)
        return jnp.concatenate([signal[offset:], zero_rows], axis=0)
    if offset < 0:
        zero_rows = jnp.zeros((-offset,) + signal.shape[1:], signal.dtype)
        return jnp.concatenate([zero_rows, signal[:offset]], axis=0)
    return signal


def utterance_ids(lengths, frames):
    utt_ends = jnp.cumsum(lengths) * STRIDE
    places = jnp.arange(frames, dtype=jnp.int32)
    return 1 + jnp.sum((places[:, None] >= utt_ends[None, :]).astype(jnp.int32), axis=1)


def stacked_taps(signal, labels, dilation, sign):
    pieces = []
    for tap_index in range(K):
        offset = sign * dilation * (tap_index - K // 2)
        same_utt = (shift_rows(labels, offset) == labels).astype(signal.dtype)
        pieces.append(shift_rows(signal, offset) * same_utt[:, None])
    return jnp.concatenate(pieces, axis=1)


def snake_parts(signal, sharpness):
    turns = signal * (sharpness * (1.0 / jnp.pi))
    turns = turns - jnp.round(turns)
    sine = jnp.sin(jnp.pi * turns)
    cosine = jnp.cos(jnp.pi * turns)
    return sine, cosine


def snake_act(signal, sharpness):
    return signal + jnp.square(jnp.sin(sharpness * signal)) / sharpness


def normalize(values, reduce_axis):
    return values * lax.rsqrt(jnp.sum(values * values, axis=reduce_axis, keepdims=True) + 1.0)


def contract_rows(left, right):
    return lax.dot_general(left, right, (((0,), (0,)), ((), ())), preferred_element_type=F32)


def contract_cols(left, right):
    return lax.dot_general(left, right, (((1,), (1,)), ((), ())), preferred_element_type=F32)


def chip_grid(count):
    bits = count.bit_length() - 1
    side = 1 << (bits // 3)
    return ((1, side), (side, side), (side * side, count // (side * side)))


def ring_pairs(count, step, size):
    pairs = []
    for index in range(count):
        place = (index // step) % size
        pairs.append((index, index + (((place + 1) % size) - place) * step))
    return pairs


def scatter_axis(part, count, step, size):
    place = (lax.axis_index("dp") // step) % size
    rows = part.shape[0] // size
    pairs = ring_pairs(count, step, size)

    def block(back):
        start = lax.rem(place + (2 * size - back), size) * rows
        return lax.dynamic_slice_in_dim(part, start, rows, 0)

    moving = block(1)
    for turn in range(size - 1):
        got = lax.ppermute(moving, "dp", pairs)
        moving = (got.astype(F32) + block(2 + turn).astype(F32)).astype(BF)
    return moving


def gather_axis(part, count, step, size):
    place = (lax.axis_index("dp") // step) % size
    rows = part.shape[0]
    pairs = ring_pairs(count, step, size)
    whole = jnp.zeros((size * rows,) + part.shape[1:], part.dtype)
    whole = lax.dynamic_update_slice_in_dim(whole, part, place * rows, 0)
    moving = part
    for turn in range(size - 1):
        moving = lax.ppermute(moving, "dp", pairs)
        start = lax.rem(place + (2 * size - 1 - turn), size) * rows
        whole = lax.dynamic_update_slice_in_dim(whole, moving, start, 0)
    return whole


def sum_over_chips(part, count, order):
    axes = [chip_grid(count)[index] for index in order]
    for step, size in axes:
        part = scatter_axis(part, count, step, size)
    for step, size in reversed(axes):
        part = gather_axis(part, count, step, size)
    return part


def sum_chunk(chunk, count):
    rows = chunk.shape[0] // 128
    third = rows // 3
    cuts = [0, (rows - third) // 2, 2 * ((rows - third) // 2), rows]
    orders = ((0, 1, 2), (1, 2, 0), (2, 0, 1))
    parts = []
    for index in range(3):
        piece = chunk[cuts[index] * 128 : cuts[index + 1] * 128]
        parts.append(sum_over_chips(piece, count, orders[index]))
    return jnp.concatenate(parts, axis=0)


def sum_small(values, count):
    for step, size in chip_grid(count):
        pairs = ring_pairs(count, step, size)
        moving = values
        total = values
        for _ in range(size - 1):
            moving = lax.ppermute(moving, "dp", pairs)
            total = total + moving
        values = total
    return values


def swap(values):
    return lax.ppermute(values, "chan", [(0, 1), (1, 0)])


def shards(
    frames_in,
    utter_lengths,
    code_ids,
    alpha_first,
    alpha_second,
    alpha_last,
    w_dilated,
    w_point,
    w_down,
    w_latent,
    w_expand,
    codebook,
    out_grad,
):
    count = lax.axis_size("dp")
    core = lax.axis_index("chan")
    frames = frames_in.shape[2]
    half = frames_in.shape[3]
    full = 2 * half
    out_frames = frames // STRIDE
    latent_width = codebook.shape[0]

    def join(mine, other, axis):
        return jnp.where(
            core == 0,
            jnp.concatenate([mine, other], axis=axis),
            jnp.concatenate([other, mine], axis=axis),
        )

    def own_half(values, axis):
        return lax.dynamic_slice_in_dim(values, core * half, half, axis)

    def other_half(values, axis):
        return lax.dynamic_slice_in_dim(values, (1 - core) * half, half, axis)

    def mine_of(values):
        return lax.dynamic_index_in_dim(values, core, 0, keepdims=False)

    def other_of(values):
        return lax.dynamic_index_in_dim(values, 1 - core, 0, keepdims=False)

    running = join(
        mine_of(frames_in)[0], swap(other_of(frames_in)[0]), 1
    ).astype(F32)
    lengths = mine_of(utter_lengths)[0]
    lengths_other = other_of(utter_lengths)[0]
    labels = utterance_ids(lengths, frames)
    labels_other = utterance_ids(lengths_other, frames)
    alphas = join(
        jnp.concatenate([alpha_first, alpha_second, alpha_last[None]], axis=0),
        swap(jnp.concatenate([alpha_first, alpha_second, alpha_last[None]], axis=0)),
        1,
    )
    w_full = [
        join(w_dilated[u], swap(w_dilated[u]), 2).reshape(K * full, full) for u in range(3)
    ]
    p_full = [join(w_point[u], swap(w_point[u]), 1) for u in range(3)]

    down_code = jnp.einsum("kco,ol->ckl", w_down, w_latent, preferred_element_type=F32)
    down_code = down_code.reshape(full, KS * latent_width)
    down_code = down_code + swap(down_code)

    ids = mine_of(code_ids)[0]
    code_range = jnp.arange(codebook.shape[1], dtype=jnp.int32)
    selector = (ids[:, None] == code_range[None, :]).astype(F32)
    code_unit, code_back = jax.vjp(lambda values: normalize(values, 0), codebook)
    chosen = lax.dot_general(
        selector, code_unit, (((1,), (1,)), ((), ())), precision=HIGHEST, preferred_element_type=F32
    )
    grad_parts = [contract_cols(out_grad[m, 0], w_expand) for m in range(2)]
    grad_parts = jnp.stack(grad_parts)
    grad_mixed = mine_of(grad_parts) + swap(other_of(grad_parts))
    code_sum = lax.dot_general(
        grad_mixed, selector, (((0,), (0,)), ((), ())), precision=HIGHEST, preferred_element_type=F32
    )

    kept = []
    for u in range(3):
        opened = snake_act(running, alphas[u]).astype(BF)
        opened_other = swap(opened)
        stacked = stacked_taps(opened, labels, DILATIONS[u], 1)
        dilated_out = jnp.dot(stacked, w_full[u], preferred_element_type=F32)
        closed = snake_act(dilated_out, alphas[3 + u]).astype(BF)
        closed_other = swap(closed)
        kept.append((running, opened, opened_other, dilated_out, closed, closed_other))
        running = running + jnp.dot(closed, p_full[u], preferred_element_type=F32)

    opened_last = snake_act(running, alphas[6]).astype(BF)
    width = KS * latent_width
    place = jnp.arange(frames, dtype=jnp.int32)[:, None] % STRIDE
    tap = jnp.arange(width, dtype=jnp.int32)[None, :] // latent_width
    pattern = (tap % STRIDE == (place + STRIDE // 2) % STRIDE).astype(F32)
    marks = labels[::STRIDE]
    same_before = (shift_rows(marks, -1) == marks).astype(F32)[:, None]
    same_after = (shift_rows(marks, 1) == marks).astype(F32)[:, None]
    lane = jnp.arange(width, dtype=jnp.int32)[None, :]
    early = lane < 4 * latent_width
    late = lane >= 12 * latent_width
    fold = (lane.T % latent_width == jnp.arange(latent_width)[None, :]).astype(F32)
    products = jnp.dot(opened_last.astype(F32), down_code, precision=HIGHEST)
    sums = jnp.sum((products * pattern).reshape(out_frames, STRIDE, width), axis=1)
    sums = jnp.where(
        early,
        same_before * shift_rows(sums, -1),
        jnp.where(late, same_after * shift_rows(sums, 1), sums),
    )
    latent = jnp.dot(sums, fold, precision=HIGHEST)
    latent_unit, latent_back = jax.vjp(lambda values: normalize(values, 1), latent)
    mixed_code = (latent_unit + chosen).astype(BF)
    mixed_other = swap(mixed_code)
    mixed_both = jnp.where(
        core == 0, jnp.stack([mixed_code, mixed_other]), jnp.stack([mixed_other, mixed_code])
    )
    block_out = jnp.einsum(
        "mjl,lo->mjo", mixed_both, w_expand, preferred_element_type=F32
    ).astype(BF)[:, None]
    expand_sum = jnp.einsum(
        "mjl,mjo->lo", mixed_both, out_grad[:, 0], preferred_element_type=F32
    )
    grad_latent = latent_back(grad_mixed)[0]
    spread = jnp.tile(grad_latent, (1, KS))
    spread = jnp.where(
        early,
        shift_rows(same_before * spread, 1),
        jnp.where(late, shift_rows(same_after * spread, -1), spread),
    )
    spread = jnp.repeat(spread, STRIDE, axis=0) * pattern
    down_sum = lax.dot_general(
        opened_last.astype(F32), spread, (((0,), (0,)), ((), ())), precision=HIGHEST
    )
    grad_last = lax.dot_general(
        spread, down_code, (((1,), (1,)), ((), ())), precision=HIGHEST
    )
    grad_running, grad_rate_last = jax.vjp(snake_act, running, alphas[6])[1](grad_last)

    rate_sums = [None] * 6 + [grad_rate_last]
    chunks = [None] * 3
    for u in (2, 1, 0):
        running_in, opened, opened_other, dilated_out, closed, closed_other = kept[u]
        grad_point = grad_running.astype(BF)
        grad_closed = contract_cols(grad_point, p_full[u])
        grad_dilated, rate = jax.vjp(snake_act, dilated_out, alphas[3 + u])[1](grad_closed)
        rate_sums[3 + u] = rate
        grad_dilated = grad_dilated.astype(BF)
        point_other = swap(other_half(grad_point, 1))
        dilated_other = swap(other_half(grad_dilated, 1))
        stacked = stacked_taps(grad_dilated, labels, DILATIONS[u], -1)
        grad_opened = contract_cols(
            stacked,
            jnp.transpose(w_full[u].reshape(K, full, full), (1, 0, 2)).reshape(full, K * full),
        )
        stacked_own = stacked_taps(own_half(grad_dilated, 1), labels, DILATIONS[u], -1)
        stacked_other = stacked_taps(dilated_other, labels_other, DILATIONS[u], -1)
        conv = contract_rows(opened, stacked_own) + contract_rows(opened_other, stacked_other)
        conv = jnp.transpose(conv.astype(BF).reshape(full, K, half), (1, 0, 2))
        point = contract_rows(closed, own_half(grad_point, 1)) + contract_rows(
            closed_other, point_other
        )
        pieces = [conv.reshape(K * full, half), point.astype(BF)]
        if u == 2:
            down_half = lax.dynamic_slice_in_dim(down_sum, core * half, half, 0) + swap(
                lax.dynamic_slice_in_dim(down_sum, (1 - core) * half, half, 0)
            )
            code_width = codebook.shape[1] // 2
            code_half = lax.dynamic_slice_in_dim(code_sum, core * code_width, code_width, 1) + swap(
                lax.dynamic_slice_in_dim(code_sum, (1 - core) * code_width, code_width, 1)
            )
            pieces += [
                down_half.astype(BF).reshape(-1, half),
                code_half.astype(BF).reshape(-1, half),
            ]
        chunks[u] = sum_chunk(jnp.concatenate(pieces, axis=0), count)
        grad_input, rate = jax.vjp(snake_act, running_in, alphas[u])[1](grad_opened)
        rate_sums[u] = rate
        grad_running = grad_running + grad_input

    rates = jnp.stack(rate_sums)
    rates = own_half(rates, 1) + swap(other_half(rates, 1))
    small = jnp.concatenate([rates, expand_sum.reshape(-1, half)], axis=0)
    small = sum_small(small, count)
    conv_rows = K * full
    w_rows = conv_rows + full
    down_rows = full * width // 2 // half
    down_half = chunks[2][w_rows : w_rows + down_rows].reshape(half, width)
    code_half = chunks[2][w_rows + down_rows :].reshape(latent_width, codebook.shape[1] // 2)
    down_total = join(down_half, swap(down_half), 0).astype(F32)
    code_total = join(code_half, swap(code_half), 1).astype(F32)
    down_taps = jnp.transpose(down_total.reshape(full, KS, latent_width), (1, 0, 2))
    grad_w_down = jnp.einsum(
        "kcl,ol->kco", down_taps, w_latent.astype(F32), preferred_element_type=F32
    )
    grad_w_latent = jnp.einsum(
        "kco,kcl->ol", w_down, down_taps.astype(BF), preferred_element_type=F32
    )
    grad_codebook = code_back(code_total)[0]

    sent = swap(other_half(grad_running, 1))
    kept_half = own_half(grad_running, 1)
    grad_frames = jnp.where(
        core == 0, jnp.stack([kept_half, sent]), jnp.stack([sent, kept_half])
    )[:, None]
    return (
        block_out,
        grad_frames,
        small[0:3],
        small[3:6],
        small[6],
        jnp.stack([chunks[u][:conv_rows] for u in range(3)])
        .astype(F32)
        .reshape(3, K, full, half),
        jnp.stack([chunks[u][conv_rows:w_rows] for u in range(3)]).astype(F32),
        grad_w_down,
        grad_w_latent,
        small[7:].reshape(latent_width, -1),
        grad_codebook,
    )


def solution(mesh):
    placed = (
        P(None, "dp", None, "chan"),
        P(None, "dp", None),
        P(None, "dp", None),
        P(None, "chan"),
        P(None, "chan"),
        P("chan"),
        P(None, None, None, "chan"),
        P(None, None, "chan"),
        P(None, None, "chan"),
        P("chan", None),
        P(None, "chan"),
        P(),
        P(None, "dp", None, "chan"),
    )
    return jax.shard_map(
        shards,
        mesh=mesh,
        in_specs=placed,
        out_specs=(
            P(None, "dp", None, "chan"),
            P(None, "dp", None, "chan"),
            P(None, "chan"),
            P(None, "chan"),
            P("chan"),
            P(None, None, None, "chan"),
            P(None, None, "chan"),
            P(None, None, "chan"),
            P("chan", None),
            P(None, "chan"),
            P(),
        ),
        check_vma=False,
    )
```

time: 1560 us -> 765 us (0.49)
  waiting for transfers between devices: 856 us -> 227 us
  other arithmetic: 167 us -> 83.6 us
  blocking collectives: 77.7 us -> 0 us
  starting transfers between devices: 4.07 us -> 75.9 us
  local copies, waits for them, and re-layouts: 161 us -> 118 us
  matrix products: 264 us -> 245 us
    psum x1 -> x0, waiting for transfers between devices: 731 us -> none  [shards(): lax.psum((jnp.stack(first_sums), jnp.stack(second_sums), jnp.stack(dilate...]
    ppermute x0 -> x124, waiting for transfers between devices: none -> 227 us  [the longest x45 111 us: gather_axis(): moving = lax.ppermute(moving, 'dp', pairs)]
    all_gather x14 -> x0, waiting for transfers between devices: 103 us -> none  [gather_channels(): return lax.all_gather(shard_part, 'chan', axis=1, tiled=True)]
    psum x2 -> x0, blocking collectives: 77.7 us -> none  [the longest x1 74.2 us: shards(): lax.psum((jnp.stack(first_sums), jnp.stack(second_sums), jnp.stack(dilate...]
    ppermute x0 -> x124, starting transfers between devices: none -> 75.9 us  [the longest x45 38.3 us: scatter_axis(): got = lax.ppermute(moving, 'dp', pairs)]
    reduce_sum x7 -> x0, other arithmetic: 75.2 us -> none  [snake_act(): return signal + jnp.square(jnp.sin(sharpness * signal)) / sharpness]
    split x24 -> x0, local copies, waits for them, and re-layouts: 56.5 us -> none  [the longest x6 53.3 us: dilated_taps(): return jnp.concatenate(pieces, axis=1)]
    unnamed x357 -> x363, local copies, waits for them, and re-layouts: 64.7 us -> 12.5 us
  transfers between devices with their start and end apart: 29 -> 124, of which waited for: 18 -> 58; matrix products, arithmetic and copies ran while one was open for 24% -> 57% of each run, Pallas kernels for 0% -> 0%
where the time goes in v1:
time: 765 us; the launch traced here: 756 us
  matrix products  245 us (32%)
  waiting for transfers between devices  227 us (30%)
  local copies, waits for them, and re-layouts  118 us (15%)
  other arithmetic  83.6 us (11%)
  starting transfers between devices  75.9 us (10%)
    ppermute x45, waiting for transfers between devices, gather_axis(): moving = lax.ppermute(moving, 'dp', pairs)  111 us
    ppermute x45, waiting for transfers between devices, scatter_axis(): got = lax.ppermute(moving, 'dp', pairs)  110 us
    dot_general x8, matrix products, contract_cols(): lax.dot_general(left, right, (((1,), (1,)), ((), ())), preferred_element_...  84 us
    dot_general x3, matrix products, shards(): dilated_out = jnp.dot(stacked, w_full[u], preferred_element_type=F32)  52.6 us
    dot_general x12, matrix products, contract_rows(): lax.dot_general(left, right, (((0,), (0,)), ((), ())), preferred_element_...  41.9 us
    ppermute x45, starting transfers between devices, scatter_axis(): got = lax.ppermute(moving, 'dp', pairs)  38.3 us
    unnamed x52, other arithmetic  30.6 us
    ppermute x45, starting transfers between devices, gather_axis(): moving = lax.ppermute(moving, 'dp', pairs)  27 us
  transfers between devices with their start and end apart: 124, of which 58 were waited for; matrix products, arithmetic and copies ran while one was open for 57% of the time, Pallas kernels for 0%

profile of v1, /device:TPU:0, one launch (start us, length us, event | category | flops | bytes accessed | tf_op | source)
XLA Modules:
  0.0 755.6 jit_solution(7214125906998223617)
XLA Ops:
  7.8 5.9 fusion.172
  22.9 5.6 convolution_bitcast_fusion
  34.1 8.0 %fusion.35 = bf16[1024,512]{1,0:T(8,128)(2,1)} fusion(f32[512]{0:T(512)S(1)} %bitcast.228, bf16[1024,256]{1,0:T(8,128)(2,1)S(1)} %get-tuple-element.202, bf16[1024,256]{1,0:T(8,128)(2,1)S(1)} %collective-permute-done, pred[]{:T(512)S(6)} %eq.273), kind=kLoop, calls=%fused_computation.50 | loop fusion | flops 7864320 | bytes 2099201 | tf_op jit(solution)/shard_map/convert_element_type | solution.py:224
  52.1 17.1 %add_convert_fusion.11 = (bf16[1024,512]{1,0:T(8,128)(2,1)}, f32[1024,512]{1,0:T(8,128)}) fusion(f32[512]{0:T(512)S(1)} %bitcast.235, bf16[1024,3584]{1,0:T(8,128)(2,1)S(1)} %multiply_dynamic-update-slice_fusion.30, bf16[3584,256]{1,0:T(8,128)(2,1)} %bitcast.8, bf16[3584,256]{1,0:T(8,128)(2,1)S(1)} %bitcast.212, pred[]{:T(512)S(6)} %eq.273), kind=kOutput, calls=%fused_computation.85 | convolution fusion | flops 3777232896 | bytes 14157825 | tf_op jit(solution)/shard_map/dot_general | solution.py:227
  69.5 9.0 %add_convert_fusion.10 = (bf16[1024,512]{1,0:T(8,128)(2,1)S(1)}, f32[1024,512]{1,0:T(8,128)S(1)}) fusion(f32[512]{0:T(512)S(1)} %bitcast.238, bf16[1024,512]{1,0:T(8,128)(2,1)} %get-tuple-element.328, bf16[512,256]{1,0:T(8,128)(2,1)} %collective-permute-done.3, bf16[512,256]{1,0:T(8,128)(2,1)S(1)} %get-tuple-element.206, pred[]{:T(512)S(6)} %eq.273, ...), kind=kOutput, calls=%fused_computation.84 | convolution fusion | flops 547618816 | bytes 5769217 | tf_op jit(solution)/shard_map/dot_general | solution.py:231
  82.0 23.0 %add_convert_fusion.9 = (bf16[1024,512]{1,0:T(8,128)(2,1)S(1)}, f32[1024,512]{1,0:T(8,128)}) fusion(f32[512]{0:T(512)S(1)} %bitcast.241, bf16[1024,3584]{1,0:T(8,128)(2,1)S(1)} %multiply_dynamic-update-slice_fusion.24, bf16[3584,256]{1,0:T(8,128)(2,1)S(1)} %bitcast.213, bf16[3584,256]{1,0:T(8,128)(2,1)S(1)} %bitcast.211, pred[]{:T(512)S(6)} %eq.273), kind=kOutput, calls=%fused_computation.83 | convolution fusion | flops 3777232896 | bytes 14157825 | tf_op jit(solution)/shard_map/dot_general | solution.py:227
  105.1 7.4 add_convert_fusion.8
  116.0 12.5 %add_convert_fusion.7 = (bf16[1024,512]{1,0:T(8,128)(2,1)}, f32[1024,512]{1,0:T(8,128)}) fusion(f32[512]{0:T(512)S(1)} %bitcast.250, bf16[1024,3584]{1,0:T(8,128)(2,1)S(1)} %multiply_dynamic-update-slice_fusion.18, bf16[3584,256]{1,0:T(8,128)(2,1)S(1)} %bitcast.214, bf16[3584,256]{1,0:T(8,128)(2,1)S(1)} %bitcast.210, pred[]{:T(512)S(6)} %eq.273), kind=kOutput, calls=%fused_computation.81 | convolution fusion | flops 3777232896 | bytes 14157825 | tf_op jit(solution)/shard_map/dot_general | solution.py:227
  128.9 10.1 %add_convert_fusion.6 = (bf16[1024,512]{1,0:T(8,128)(2,1)S(1)}, f32[1024,512]{1,0:T(8,128)}) fusion(f32[512]{0:T(512)S(1)} %bitcast.244, f32[1024,512]{1,0:T(8,128)S(1)} %get-tuple-element.335, bf16[1024,512]{1,0:T(8,128)(2,1)} %get-tuple-element.336, bf16[512,256]{1,0:T(8,128)(2,1)S(1)} %collective-permute-done.7, bf16[512,256]{1,0:T(8,128)(2,1)S(1)} %copy-done.69, ...), kind=kOutput, calls=%fused_computation.80 | convolution fusion | flops 542375936 | bytes 6817793 | tf_op jit(solution)/shard_map/dot_general | solution.py:231
  142.9 13.0 %multiply_reduce_fusion.1 = (f32[512]{0:T(512)}, f32[512]{0:T(512)}, bf16[1024,512]{1,0:T(8,128)(2,1)S(1)}, f32[1024,512]{1,0:T(8,128)}) fusion(f32[1024,512]{1,0:T(8,128)} %get-tuple-element.339, f32[512]{0:T(512)S(1)} %bitcast.252, f32[512]{0:T(512)S(1)} %bitcast.245, f32[512,128]{0,1:T(8,128)} %copy-done.55, f32[128,128]{1,0:T(8,128)S(1)} %select_select_fusion, ...), kind=kOutput, calls=%fused_computation.54 | convolution fusion | flops 812907520 | bytes 5583360 | tf_op jit(solution)/shard_map/dot_general | solution.py:276
  155.9 9.3 %multiply_reduce_fusion.3 = (f32[512]{0:T(512)}, f32[512]{0:T(512)}, bf16[1024,512]{1,0:T(8,128)(2,1)S(1)}) fusion(f32[1024,512]{1,0:T(8,128)S(1)} %copy-done.176, f32[512]{0:T(512)S(1)} %bitcast.249, f32[512]{0:T(512)S(1)} %bitcast.251, bf16[1024,512]{1,0:T(8,128)(2,1)S(1)} %get-tuple-element.124, bf16[512,256]{1,0:T(8,128)(2,1)S(1)} %copy-done.164, ...), kind=kOutput, calls=%fused_computation.56 | convolution fusion | flops 546569216 | bytes 4726785 | tf_op jit(solution)/shard_map/dot_general | solution.py:61
  175.3 6.3 copy.92
  187.3 23.6 %multiply_reduce_fusion.9 = (f32[512]{0:T(512)}, f32[512]{0:T(512)}, bf16[1024,512]{1,0:T(8,128)(2,1)S(1)}, f32[1024,512]{1,0:T(8,128)}) fusion(f32[1024,512]{1,0:T(8,128)} %copy-done.173, f32[512]{0:T(512)S(1)} %bitcast.243, f32[512]{0:T(512)S(1)} %bitcast.248, f32[1024,512]{1,0:T(8,128)} %get-tuple-element.341, f32[1024,512]{1,0:T(8,128)} %get-tuple-element.339, ...), kind=kOutput, calls=%fused_computation.62 | convolution fusion | flops 3769629696 | bytes 20457472 | tf_op jit(solution)/shard_map/dot_general | solution.py:61
  210.9 9.3 %multiply_reduce_fusion.5 = (f32[512]{0:T(512)}, f32[512]{0:T(512)}, bf16[1024,512]{1,0:T(8,128)(2,1)S(1)}) fusion(f32[1024,512]{1,0:T(8,128)S(1)} %copy-done.175, f32[512]{0:T(512)S(1)} %bitcast.240, f32[512]{0:T(512)S(1)} %bitcast.242, bf16[1024,512]{1,0:T(8,128)(2,1)S(1)} %get-tuple-element.128, bf16[512,256]{1,0:T(8,128)(2,1)S(1)} %copy-done.162, ...), kind=kOutput, calls=%fused_computation.58 | convolution fusion | flops 546569216 | bytes 4726785 | tf_op jit(solution)/shard_map/dot_general | solution.py:61
  236.5 6.2 copy.93
  248.4 15.2 %multiply_reduce_fusion.11 = (f32[512]{0:T(512)}, f32[512]{0:T(512)}, bf16[1024,512]{1,0:T(8,128)(2,1)S(1)}, f32[1024,512]{1,0:T(8,128)}) fusion(f32[1024,512]{1,0:T(8,128)S(1)} %copy-done.172, f32[512]{0:T(512)S(1)} %bitcast.237, f32[512]{0:T(512)S(1)} %bitcast.239, f32[1024,512]{1,0:T(8,128)} %get-tuple-element.129, ...), kind=kOutput, calls=%fused_computation.64 | convolution fusion | flops 3765959680 | bytes 18358272 | tf_op jit(solution)/shard_map/dot_general | solution.py:61
  263.7 10.4 %multiply_reduce_fusion.7 = (f32[512]{0:T(512)}, f32[512]{0:T(512)}, bf16[1024,512]{1,0:T(8,128)(2,1)S(1)}) fusion(f32[1024,512]{1,0:T(8,128)S(1)} %copy-done.174, f32[512]{0:T(512)S(1)} %bitcast.234, f32[512]{0:T(512)S(1)} %bitcast.236, bf16[1024,512]{1,0:T(8,128)(2,1)S(1)} %get-tuple-element.130, bf16[512,256]{1,0:T(8,128)(2,1)} %collective-permute-done.3, ...), kind=kOutput, calls=%fused_computation.60 | convolution fusion | flops 546569216 | bytes 4726785 | tf_op jit(solution)/shard_map/dot_general | solution.py:61
  307.3 6.4 copy.94
  318.6 13.9 %fusion.32 = (f32[512]{0:T(512)S(1)}, f32[512]{0:T(512)S(1)}, f32[1024,512]{1,0:T(8,128)S(1)}) fusion(f32[512]{0:T(512)S(1)} %bitcast.233, f32[512]{0:T(512)S(1)} %bitcast.229, bf16[1024,256]{1,0:T(8,128)(2,1)S(1)} %copy-done.29, bf16[1024,256]{1,0:T(8,128)(2,1)S(1)} %copy-done.52, pred[]{:T(512)S(6)} %eq.273, f32[1024,512]{1,0:T(8,128)} %get-tuple-element.131, ...), kind=kOutput, calls=%fused_computation.47 | convolution fusion | flops 3770678272 | bytes 16261121 | tf_op jit(solution)/shard_map/dot_general | solution.py:61
  334.7 6.1 fusion.222
  340.8 5.2 fusion.221
  409.5 5.6 add_convert_fusion.1
  446.7 6.3 collective-permute-done.33
  453.0 5.8 collective-permute-done.23
  462.9 6.2 collective-permute-done.24
  470.5 7.0 collective-permute-done.42
  482.2 6.0 collective-permute-done.25
  488.3 5.8 collective-permute-done.26
  494.1 6.3 collective-permute-done.36
  500.5 5.8 collective-permute-done.27
  506.4 8.9 %collective-permute-done.77 = bf16[320,256]{1,0:T(8,128)(2,1)S(1)} collective-permute-done((bf16[320,256]{1,0:T(8,128)(2,1)S(1)}, bf16[320,256]{1,0:T(8,128)(2,1)S(1)}, u32[]{:S(2)}, u32[]{:S(2)}) %collective-permute-start.77) | collective-permute-done | bytes 163872 | tf_op jit(solution)/shard_map/ppermute | solution.py:89
  515.4 6.9 collective-permute-done.43
  533.2 5.9 collective-permute-done.99
  539.1 6.3 collective-permute-done.65
  545.4 6.3 collective-permute-done.38
  583.5 5.8 collective-permute-done.91
  589.3 5.8 collective-permute-done.57
  612.8 6.2 collective-permute-done.93
  619.1 6.2 collective-permute-done.59
  646.0 5.8 collective-permute-done.95
  651.8 5.8 collective-permute-done.61
  674.2 5.4 collective-permute-done.106
  684.2 6.0 collective-permute-done.51
  691.1 6.2 collective-permute-done.85
  698.1 6.7 collective-permute-done.120
  706.6 5.9 collective-permute-done.121
  733.5 8.5 %fusion.99 = f32[16,512,512]{2,1,0:T(8,128)} fusion(bf16[256,16,8]{0,2,1:T(8,128)(2,1)S(1)} %bitcast.215, bf16[256,16,8]{0,2,1:T(8,128)(2,1)S(1)} %copy.102, pred[]{:T(512)S(6)} %eq.273, bf16[512,8]{0,1:T(8,128)(2,1)S(1)} %copy-done), kind=kOutput, calls=%fused_computation.479 | convolution fusion | flops 67698688 | bytes 16916480 | tf_op jit(solution)/shard_map/kcl,ol->kco/dot_general | solution.py:334
  742.1 5.2 convolution_bitcast_fusion.1
  (981 shorter events, 357.7 us)
Async XLA Ops:
  3.4 136.7 %collective-permute-start.10 = (f32[128,8]{0,1:T(8,128)}, f32[128,8]{0,1:T(8,128)}, u32[]{:S(2)}, u32[]{:S(2)}) collective-permute-start(f32[128,8]{0,1:T(8,128)} %fusion.115), channel_id=1, source_target_pairs={{0,1},{1,0},{2,3},{3,2},{4,5},{5,4},{6,7},{7,6},{8,9},{9,8},{10,11... | collective-permute-start | bytes 12296 | tf_op jit(solution)/shard_map/ppermute | solution.py:142
  5.2 26.6 %collective-permute-start.1 = (f32[7,256]{1,0:T(8,128)}, f32[7,256]{1,0:T(8,128)}, u32[]{:S(2)}, u32[]{:S(2)}) collective-permute-start(f32[7,256]{1,0:T(8,128)} %pad_maximum_fusion.10), channel_id=1, source_target_pairs={{0,1},{1,0},{2,3},{3,2},{4,5},{5,4},{6,7},{7,6},{8,9},{9,8},{10,11... | collective-permute-start | bytes 21512 | tf_op jit(solution)/shard_map/ppermute | solution.py:142
  7.3 26.5 %collective-permute-start = (bf16[1024,256]{1,0:T(8,128)(2,1)}, bf16[1024,256]{1,0:T(8,128)(2,1)S(1)}, u32[]{:S(2)}, u32[]{:S(2)}) collective-permute-start(bf16[1024,256]{1,0:T(8,128)(2,1)} %get-tuple-element.201), channel_id=1, source_target_pairs={{0,1},{1,0},{2,3},{3,2},{4,5},{5,4},{6,7},{7,6},{8,9},{9,8},{10,11... | collective-permute-start | bytes 1572872 | tf_op jit(solution)/shard_map/ppermute | solution.py:142
  13.7 37.3 %collective-permute-start.2 = (bf16[7,512,256]{2,1,0:T(8,128)(2,1)S(1)}, bf16[7,512,256]{2,1,0:T(8,128)(2,1)}, u32[]{:S(2)}, u32[]{:S(2)}) collective-permute-start(bf16[7,512,256]{2,1,0:T(8,128)(2,1)S(1)} %get-tuple-element.119), channel_id=1, source_target_pairs={{0,1},{1,0},{2,3},{3,2},{4,5},{5,4},{6,7},{7,6},{8,9},{9,8},{10,11... | collective-permute-start | bytes 5505032 | tf_op jit(solution)/shard_map/ppermute | solution.py:142
  15.1 54.1 %collective-permute-start.3 = (bf16[512,256]{1,0:T(8,128)(2,1)S(1)}, bf16[512,256]{1,0:T(8,128)(2,1)}, u32[]{:S(2)}, u32[]{:S(2)}) collective-permute-start(bf16[512,256]{1,0:T(8,128)(2,1)S(1)} %get-tuple-element.206), channel_id=1, source_target_pairs={{0,1},{1,0},{2,3},{3,2},{4,5},{5,4},{6,7},{7,6},{8,9},{9,8},{10,11... | collective-permute-start | bytes 786440 | tf_op jit(solution)/shard_map/ppermute | solution.py:142
  33.4 47.9 %collective-permute-start.4 = (bf16[7,512,256]{2,1,0:T(8,128)(2,1)}, bf16[7,512,256]{2,1,0:T(8,128)(2,1)S(1)}, u32[]{:S(2)}, u32[]{:S(2)}) collective-permute-start(bf16[7,512,256]{2,1,0:T(8,128)(2,1)} %get-tuple-element.120), channel_id=1, source_target_pairs={{0,1},{1,0},{2,3},{3,2},{4,5},{5,4},{6,7},{7,6},{8,9},{9,8},{10,11... | collective-permute-start | bytes 5505032 | tf_op jit(solution)/shard_map/ppermute | solution.py:142
  33.8 71.2 %collective-permute-start.5 = (bf16[512,256]{1,0:T(8,128)(2,1)}, bf16[512,256]{1,0:T(8,128)(2,1)S(1)}, u32[]{:S(2)}, u32[]{:S(2)}) collective-permute-start(bf16[512,256]{1,0:T(8,128)(2,1)} %get-tuple-element.207), channel_id=1, source_target_pairs={{0,1},{1,0},{2,3},{3,2},{4,5},{5,4},{6,7},{7,6},{8,9},{9,8},{10,11... | collective-permute-start | bytes 786440 | tf_op jit(solution)/shard_map/ppermute | solution.py:142
  51.6 63.9 %collective-permute-start.6 = (bf16[7,512,256]{2,1,0:T(8,128)(2,1)S(1)}, bf16[7,512,256]{2,1,0:T(8,128)(2,1)S(1)}, u32[]{:S(2)}, u32[]{:S(2)}) collective-permute-start(bf16[7,512,256]{2,1,0:T(8,128)(2,1)S(1)} %copy-done.10), channel_id=1, source_target_pairs={{0,1},{1,0},{2,3},{3,2},{4,5},{5,4},{6,7},{7,6},{8,9},{9,8},{10,11... | collective-permute-start | bytes 5505032 | tf_op jit(solution)/shard_map/ppermute | solution.py:142
  69.2 59.6 %collective-permute-start.7 = (bf16[512,256]{1,0:T(8,128)(2,1)S(1)}, bf16[512,256]{1,0:T(8,128)(2,1)S(1)}, u32[]{:S(2)}, u32[]{:S(2)}) collective-permute-start(bf16[512,256]{1,0:T(8,128)(2,1)S(1)} %copy-done.69), channel_id=1, source_target_pairs={{0,1},{1,0},{2,3},{3,2},{4,5},{5,4},{6,7},{7,6},{8,9},{9,8},{10,11... | collective-permute-start | bytes 786440 | tf_op jit(solution)/shard_map/ppermute | solution.py:142
  81.4 280.1 %collective-permute-start.18 = (bf16[1024,512]{1,0:T(8,128)(2,1)}, bf16[1024,512]{1,0:T(8,128)(2,1)}, u32[]{:S(2)}, u32[]{:S(2)}) collective-permute-start(bf16[1024,512]{1,0:T(8,128)(2,1)} %fusion.35), channel_id=1, source_target_pairs={{0,1},{1,0},{2,3},{3,2},{4,5},{5,4},{6,7},{7,6},{8,9},{9,8},{10,11... | collective-permute-start | bytes 3145736 | tf_op jit(solution)/shard_map/ppermute | solution.py:142
  128.5 295.9 %collective-permute-start.108 = (bf16[1024,512]{1,0:T(8,128)(2,1)}, bf16[1024,512]{1,0:T(8,128)(2,1)}, u32[]{:S(2)}, u32[]{:S(2)}) collective-permute-start(bf16[1024,512]{1,0:T(8,128)(2,1)} %get-tuple-element.336), channel_id=1, source_target_pairs={{0,1},{1,0},{2,3},{3,2},{4,5},{5,4},{6,7},{7,6},{8,9},{9,8},{10,11... | collective-permute-start | bytes 3145736 | tf_op jit(solution)/shard_map/ppermute | solution.py:142
  229.2 167.7 %collective-permute-start.86 = (bf16[1024,512]{1,0:T(8,128)(2,1)S(1)}, bf16[1024,512]{1,0:T(8,128)(2,1)}, u32[]{:S(2)}, u32[]{:S(2)}) collective-permute-start(bf16[1024,512]{1,0:T(8,128)(2,1)S(1)} %get-tuple-element.334), channel_id=1, source_target_pairs={{0,1},{1,0},{2,3},{3,2},{4,5},{5,4},{6,7},{7,6},{8,9},{9,8},{10,11... | collective-permute-start | bytes 3145736 | tf_op jit(solution)/shard_map/ppermute | solution.py:142
  286.7 60.3 %collective-permute-start.111 = (f32[8,4096]{1,0:T(8,128)}, f32[8,4096]{1,0:T(8,128)S(1)}, u32[]{:S(2)}, u32[]{:S(2)}) collective-permute-start(f32[8,4096]{1,0:T(8,128)} %constant_dynamic-slice_fusion.14), channel_id=1, source_target_pairs={{0,1},{1,0},{2,3},{3,2},{4,5},{5,4},{6,7},{7,6},{8,9},{9,8},{10,11... | collective-permute-start | bytes 393224 | tf_op jit(solution)/shard_map/ppermute | solution.py:142
  348.8 78.6 %collective-permute-start.74 = (bf16[1024,512]{1,0:T(8,128)(2,1)}, bf16[1024,512]{1,0:T(8,128)(2,1)}, u32[]{:S(2)}, u32[]{:S(2)}) collective-permute-start(bf16[1024,512]{1,0:T(8,128)(2,1)} %copy-done.159), channel_id=1, source_target_pairs={{0,1},{1,0},{2,3},{3,2},{4,5},{5,4},{6,7},{7,6},{8,9},{9,8},{10,11... | collective-permute-start | bytes 3145736 | tf_op jit(solution)/shard_map/ppermute | solution.py:142
  388.4 21.1 %collective-permute-start.52 = (bf16[1024,512]{1,0:T(8,128)(2,1)S(1)}, bf16[1024,512]{1,0:T(8,128)(2,1)}, u32[]{:S(2)}, u32[]{:S(2)}) collective-permute-start(bf16[1024,512]{1,0:T(8,128)(2,1)S(1)} %copy-done.2), channel_id=1, source_target_pairs={{0,1},{1,0},{2,3},{3,2},{4,5},{5,4},{6,7},{7,6},{8,9},{9,8},{10,11... | collective-permute-start | bytes 3145736 | tf_op jit(solution)/shard_map/ppermute | solution.py:142
  396.2 34.7 %collective-permute-start.40 = (bf16[1024,512]{1,0:T(8,128)(2,1)}, bf16[1024,512]{1,0:T(8,128)(2,1)}, u32[]{:S(2)}, u32[]{:S(2)}) collective-permute-start(bf16[1024,512]{1,0:T(8,128)(2,1)} %get-tuple-element.328), channel_id=1, source_target_pairs={{0,1},{1,0},{2,3},{3,2},{4,5},{5,4},{6,7},{7,6},{8,9},{9,8},{10,11... | collective-permute-start | bytes 3145736 | tf_op jit(solution)/shard_map/ppermute | solution.py:142
  396.9 26.9 %collective-permute-start.109 = (bf16[1024,256]{1,0:T(8,128)(2,1)}, bf16[1024,256]{1,0:T(8,128)(2,1)}, u32[]{:S(2)}, u32[]{:S(2)}) collective-permute-start(bf16[1024,256]{1,0:T(8,128)(2,1)} %constant_dynamic-slice_fusion.16), channel_id=1, source_target_pairs={{0,1},{1,0},{2,3},{3,2},{4,5},{5,4},{6,7},{7,6},{8,9},{9,8},{10,11... | collective-permute-start | bytes 1572872 | tf_op jit(solution)/shard_map/ppermute | solution.py:142
  409.5 24.5 %collective-permute-start.11 = (f32[1024,256]{1,0:T(8,128)}, f32[1024,256]{1,0:T(8,128)}, u32[]{:S(2)}, u32[]{:S(2)}) collective-permute-start(f32[1024,256]{1,0:T(8,128)} %get-tuple-element.134), channel_id=1, source_target_pairs={{0,1},{1,0},{2,3},{3,2},{4,5},{5,4},{6,7},{7,6},{8,9},{9,8},{10,11... | collective-permute-start | bytes 3145736 | tf_op jit(solution)/shard_map/ppermute | solution.py:142
  427.5 13.0 %collective-permute-start.32 = (bf16[176,256]{1,0:T(8,128)(2,1)S(1)}, bf16[176,256]{1,0:T(8,128)(2,1)S(1)}, u32[]{:S(2)}, u32[]{:S(2)}) collective-permute-start(bf16[176,256]{1,0:T(8,128)(2,1)S(1)} %copy-done.73), channel_id=1, source_target_pairs={{0,8},{2,10},{4,12},{6,14},{8,16},{10,18},{12,20},{14,22},{16,24},... | collective-permute-start | bytes 270344 | tf_op jit(solution)/shard_map/ppermute | solution.py:89
  429.6 52.5 %collective-permute-start.112 = (bf16[384,256]{1,0:T(8,128)(2,1)S(1)}, bf16[384,256]{1,0:T(8,128)(2,1)S(1)}, u32[]{:S(2)}, u32[]{:S(2)}) collective-permute-start(bf16[384,256]{1,0:T(8,128)(2,1)S(1)} %constant_dynamic-slice_fusion.13), channel_id=1, source_target_pairs={{0,8},{2,10},{4,12},{6,14},{8,16},{10,18},{12,20},{14,22},{16,24},... | collective-permute-start | bytes 589832 | tf_op jit(solution)/shard_map/ppermute | solution.py:89
  431.0 91.8 %collective-permute-start.98 = (bf16[704,256]{1,0:T(8,128)(2,1)S(1)}, bf16[704,256]{1,0:T(8,128)(2,1)S(1)}, u32[]{:S(2)}, u32[]{:S(2)}) collective-permute-start(bf16[704,256]{1,0:T(8,128)(2,1)S(1)} %constant_dynamic-slice_fusion.20), channel_id=1, source_target_pairs={{0,4},{2,6},{4,0},{6,2},{8,12},{10,14},{12,8},{14,10},{16,20},{18,... | collective-permute-start | bytes 1081352 | tf_op jit(solution)/shard_map/ppermute | solution.py:89
  434.0 88.5 %collective-permute-start.88 = (bf16[704,256]{1,0:T(8,128)(2,1)S(1)}, bf16[704,256]{1,0:T(8,128)(2,1)S(1)}, u32[]{:S(2)}, u32[]{:S(2)}) collective-permute-start(bf16[704,256]{1,0:T(8,128)(2,1)S(1)} %constant_dynamic-slice_fusion.26), channel_id=1, source_target_pairs={{0,2},{2,0},{4,6},{6,4},{8,10},{10,8},{12,14},{14,12},{16,18},{18,... | collective-permute-start | bytes 1081352 | tf_op jit(solution)/shard_map/ppermute | solution.py:89
  438.7 31.3 %collective-permute-start.76 = (bf16[320,256]{1,0:T(8,128)(2,1)S(1)}, bf16[320,256]{1,0:T(8,128)(2,1)S(1)}, u32[]{:S(2)}, u32[]{:S(2)}) collective-permute-start(bf16[320,256]{1,0:T(8,128)(2,1)S(1)} %fusion.71), channel_id=1, source_target_pairs={{0,8},{2,10},{4,12},{6,14},{8,16},{10,18},{12,20},{14,22},{16,24},... | collective-permute-start | bytes 491528 | tf_op jit(solution)/shard_map/ppermute | solution.py:89
  469.1 55.9 %collective-permute-start.64 = (bf16[704,256]{1,0:T(8,128)(2,1)S(1)}, bf16[704,256]{1,0:T(8,128)(2,1)S(1)}, u32[]{:S(2)}, u32[]{:S(2)}) collective-permute-start(bf16[704,256]{1,0:T(8,128)(2,1)S(1)} %constant_dynamic-slice_fusion.35), channel_id=1, source_target_pairs={{0,4},{2,6},{4,0},{6,2},{8,12},{10,14},{12,8},{14,10},{16,20},{18,... | collective-permute-start | bytes 1081352 | tf_op jit(solution)/shard_map/ppermute | solution.py:89
  481.6 42.6 %collective-permute-start.54 = (bf16[704,256]{1,0:T(8,128)(2,1)S(1)}, bf16[704,256]{1,0:T(8,128)(2,1)S(1)}, u32[]{:S(2)}, u32[]{:S(2)}) collective-permute-start(bf16[704,256]{1,0:T(8,128)(2,1)S(1)} %constant_dynamic-slice_fusion.41), channel_id=1, source_target_pairs={{0,2},{2,0},{4,6},{6,4},{8,10},{10,8},{12,14},{14,12},{16,18},{18,... | collective-permute-start | bytes 1081352 | tf_op jit(solution)/shard_map/ppermute | solution.py:89
  522.7 30.6 %collective-permute-start.28 = (bf16[352,256]{1,0:T(8,128)(2,1)S(1)}, bf16[352,256]{1,0:T(8,128)(2,1)S(1)}, u32[]{:S(2)}, u32[]{:S(2)}) collective-permute-start(bf16[352,256]{1,0:T(8,128)(2,1)S(1)} %constant_dynamic-update-slice_fusion.77), channel_id=1, source_target_pairs={{0,4},{2,6},{4,0},{6,2},{8,12},{10,14},{12,8},{14,10},{16,20},{18,... | collective-permute-start | bytes 540680 | tf_op jit(solution)/shard_map/ppermute | solution.py:102
  524.2 29.3 %collective-permute-start.78 = (bf16[320,256]{1,0:T(8,128)(2,1)S(1)}, bf16[320,256]{1,0:T(8,128)(2,1)S(1)}, u32[]{:S(2)}, u32[]{:S(2)}) collective-permute-start(bf16[320,256]{1,0:T(8,128)(2,1)S(1)} %add_convert_fusion.25), channel_id=1, source_target_pairs={{0,8},{2,10},{4,12},{6,14},{8,16},{10,18},{12,20},{14,22},{16,24},... | collective-permute-start | bytes 491528 | tf_op jit(solution)/shard_map/ppermute | solution.py:89
  525.1 28.7 %collective-permute-start.44 = (bf16[320,256]{1,0:T(8,128)(2,1)S(1)}, bf16[320,256]{1,0:T(8,128)(2,1)S(1)}, u32[]{:S(2)}, u32[]{:S(2)}) collective-permute-start(bf16[320,256]{1,0:T(8,128)(2,1)S(1)} %add_convert_fusion.28), channel_id=1, source_target_pairs={{0,8},{2,10},{4,12},{6,14},{8,16},{10,18},{12,20},{14,22},{16,24},... | collective-permute-start | bytes 491528 | tf_op jit(solution)/shard_map/ppermute | solution.py:89
  531.8 22.9 %collective-permute-start.89 = (bf16[352,256]{1,0:T(8,128)(2,1)S(1)}, bf16[352,256]{1,0:T(8,128)(2,1)S(1)}, u32[]{:S(2)}, u32[]{:S(2)}) collective-permute-start(bf16[352,256]{1,0:T(8,128)(2,1)S(1)} %constant_dynamic-slice_fusion.25), channel_id=1, source_target_pairs={{0,4},{2,6},{4,0},{6,2},{8,12},{10,14},{12,8},{14,10},{16,20},{18,... | collective-permute-start | bytes 540680 | tf_op jit(solution)/shard_map/ppermute | solution.py:89
  553.3 22.0 %collective-permute-start.114 = (bf16[384,256]{1,0:T(8,128)(2,1)S(1)}, bf16[384,256]{1,0:T(8,128)(2,1)S(1)}, u32[]{:S(2)}, u32[]{:S(2)}) collective-permute-start(bf16[384,256]{1,0:T(8,128)(2,1)S(1)} %add_convert_fusion.19), channel_id=1, source_target_pairs={{0,8},{2,10},{4,12},{6,14},{8,16},{10,18},{12,20},{14,22},{16,24},... | collective-permute-start | bytes 589832 | tf_op jit(solution)/shard_map/ppermute | solution.py:89
  554.7 104.2 %collective-permute-start.39 = (bf16[704,256]{1,0:T(8,128)(2,1)S(1)}, bf16[704,256]{1,0:T(8,128)(2,1)S(1)}, u32[]{:S(2)}, u32[]{:S(2)}) collective-permute-start(bf16[704,256]{1,0:T(8,128)(2,1)S(1)} %constant_dynamic-update-slice_fusion.67), channel_id=1, source_target_pairs={{0,4},{2,6},{4,0},{6,2},{8,12},{10,14},{12,8},{14,10},{16,20},{18,... | collective-permute-start | bytes 1081352 | tf_op jit(solution)/shard_map/ppermute | solution.py:102
  557.2 103.0 %collective-permute-start.29 = (bf16[704,256]{1,0:T(8,128)(2,1)S(1)}, bf16[704,256]{1,0:T(8,128)(2,1)S(1)}, u32[]{:S(2)}, u32[]{:S(2)}) collective-permute-start(bf16[704,256]{1,0:T(8,128)(2,1)S(1)} %constant_dynamic-update-slice_fusion.75), channel_id=1, source_target_pairs={{0,2},{2,0},{4,6},{6,4},{8,10},{10,8},{12,14},{14,12},{16,18},{18,... | collective-permute-start | bytes 1081352 | tf_op jit(solution)/shard_map/ppermute | solution.py:102
  572.6 23.6 %collective-permute-start.101 = (bf16[176,256]{1,0:T(8,128)(2,1)S(1)}, bf16[176,256]{1,0:T(8,128)(2,1)S(1)}, u32[]{:S(2)}, u32[]{:S(2)}) collective-permute-start(bf16[176,256]{1,0:T(8,128)(2,1)S(1)} %add_convert_fusion.32), channel_id=1, source_target_pairs={{0,8},{2,10},{4,12},{6,14},{8,16},{10,18},{12,20},{14,22},{16,24},... | collective-permute-start | bytes 270344 | tf_op jit(solution)/shard_map/ppermute | solution.py:89
  575.3 22.7 %collective-permute-start.67 = (bf16[176,256]{1,0:T(8,128)(2,1)S(1)}, bf16[176,256]{1,0:T(8,128)(2,1)S(1)}, u32[]{:S(2)}, u32[]{:S(2)}) collective-permute-start(bf16[176,256]{1,0:T(8,128)(2,1)S(1)} %add_convert_fusion.35), channel_id=1, source_target_pairs={{0,8},{2,10},{4,12},{6,14},{8,16},{10,18},{12,20},{14,22},{16,24},... | collective-permute-start | bytes 270344 | tf_op jit(solution)/shard_map/ppermute | solution.py:89
  595.1 17.6 %collective-permute-start.115 = (bf16[192,256]{1,0:T(8,128)(2,1)S(1)}, bf16[192,256]{1,0:T(8,128)(2,1)S(1)}, u32[]{:S(2)}, u32[]{:S(2)}) collective-permute-start(bf16[192,256]{1,0:T(8,128)(2,1)S(1)} %constant_dynamic-slice_fusion.12), channel_id=1, source_target_pairs={{0,2},{2,0},{4,6},{6,4},{8,10},{10,8},{12,14},{14,12},{16,18},{18,... | collective-permute-start | bytes 294920 | tf_op jit(solution)/shard_map/ppermute | solution.py:89
  610.1 24.3 %collective-permute-start.82 = (bf16[160,256]{1,0:T(8,128)(2,1)S(1)}, bf16[160,256]{1,0:T(8,128)(2,1)S(1)}, u32[]{:S(2)}, u32[]{:S(2)}) collective-permute-start(bf16[160,256]{1,0:T(8,128)(2,1)S(1)} %constant_dynamic-update-slice_fusion.39), channel_id=1, source_target_pairs={{0,2},{2,0},{4,6},{6,4},{8,10},{10,8},{12,14},{14,12},{16,18},{18,... | collective-permute-start | bytes 245768 | tf_op jit(solution)/shard_map/ppermute | solution.py:102
  612.3 22.3 %collective-permute-start.48 = (bf16[160,256]{1,0:T(8,128)(2,1)S(1)}, bf16[160,256]{1,0:T(8,128)(2,1)S(1)}, u32[]{:S(2)}, u32[]{:S(2)}) collective-permute-start(bf16[160,256]{1,0:T(8,128)(2,1)S(1)} %constant_dynamic-update-slice_fusion.63), channel_id=1, source_target_pairs={{0,2},{2,0},{4,6},{6,4},{8,10},{10,8},{12,14},{14,12},{16,18},{18,... | collective-permute-start | bytes 245768 | tf_op jit(solution)/shard_map/ppermute | solution.py:102
  638.0 19.7 %collective-permute-start.104 = (bf16[176,256]{1,0:T(8,128)(2,1)S(1)}, bf16[176,256]{1,0:T(8,128)(2,1)S(1)}, u32[]{:S(2)}, u32[]{:S(2)}) collective-permute-start(bf16[176,256]{1,0:T(8,128)(2,1)S(1)} %constant_dynamic-update-slice_fusion.23), channel_id=1, source_target_pairs={{0,8},{2,10},{4,12},{6,14},{8,16},{10,18},{12,20},{14,22},{16,24},... | collective-permute-start | bytes 270344 | tf_op jit(solution)/shard_map/ppermute | solution.py:102
  640.8 16.9 %collective-permute-start.70 = (bf16[176,256]{1,0:T(8,128)(2,1)S(1)}, bf16[176,256]{1,0:T(8,128)(2,1)S(1)}, u32[]{:S(2)}, u32[]{:S(2)}) collective-permute-start(bf16[176,256]{1,0:T(8,128)(2,1)S(1)} %constant_dynamic-update-slice_fusion.47), channel_id=1, source_target_pairs={{0,8},{2,10},{4,12},{6,14},{8,16},{10,18},{12,20},{14,22},{16,24},... | collective-permute-start | bytes 270344 | tf_op jit(solution)/shard_map/ppermute | solution.py:102
  659.0 13.1 %collective-permute-start.96 = (bf16[352,256]{1,0:T(8,128)(2,1)S(1)}, bf16[352,256]{1,0:T(8,128)(2,1)S(1)}, u32[]{:S(2)}, u32[]{:S(2)}) collective-permute-start(bf16[352,256]{1,0:T(8,128)(2,1)S(1)} %constant_dynamic-update-slice_fusion.29), channel_id=1, source_target_pairs={{0,4},{2,6},{4,0},{6,2},{8,12},{10,14},{12,8},{14,10},{16,20},{18,... | collective-permute-start | bytes 540680 | tf_op jit(solution)/shard_map/ppermute | solution.py:102
  660.2 12.8 %collective-permute-start.62 = (bf16[352,256]{1,0:T(8,128)(2,1)S(1)}, bf16[352,256]{1,0:T(8,128)(2,1)S(1)}, u32[]{:S(2)}, u32[]{:S(2)}) collective-permute-start(bf16[352,256]{1,0:T(8,128)(2,1)S(1)} %constant_dynamic-update-slice_fusion.53), channel_id=1, source_target_pairs={{0,4},{2,6},{4,0},{6,2},{8,12},{10,14},{12,8},{14,10},{16,20},{18,... | collective-permute-start | bytes 540680 | tf_op jit(solution)/shard_map/ppermute | solution.py:102
  667.6 15.5 %collective-permute-start.119 = (bf16[384,256]{1,0:T(8,128)(2,1)S(1)}, bf16[384,256]{1,0:T(8,128)(2,1)S(1)}, u32[]{:S(2)}, u32[]{:S(2)}) collective-permute-start(bf16[384,256]{1,0:T(8,128)(2,1)S(1)} %constant_dynamic-update-slice_fusion.13), channel_id=1, source_target_pairs={{0,8},{2,10},{4,12},{6,14},{8,16},{10,18},{12,20},{14,22},{16,24},... | collective-permute-start | bytes 589832 | tf_op jit(solution)/shard_map/ppermute | solution.py:102
  668.8 14.2 %collective-permute-start.84 = (bf16[320,256]{1,0:T(8,128)(2,1)S(1)}, bf16[320,256]{1,0:T(8,128)(2,1)S(1)}, u32[]{:S(2)}, u32[]{:S(2)}) collective-permute-start(bf16[320,256]{1,0:T(8,128)(2,1)S(1)} %collective-permute-done.83), channel_id=1, source_target_pairs={{0,8},{2,10},{4,12},{6,14},{8,16},{10,18},{12,20},{14,22},{16,24},... | collective-permute-start | bytes 491528 | tf_op jit(solution)/shard_map/ppermute | solution.py:102
  679.6 25.5 %collective-permute-start.97 = (bf16[704,256]{1,0:T(8,128)(2,1)S(1)}, bf16[704,256]{1,0:T(8,128)(2,1)S(1)}, u32[]{:S(2)}, u32[]{:S(2)}) collective-permute-start(bf16[704,256]{1,0:T(8,128)(2,1)S(1)} %constant_dynamic-update-slice_fusion.27), channel_id=1, source_target_pairs={{0,2},{2,0},{4,6},{6,4},{8,10},{10,8},{12,14},{14,12},{16,18},{18,... | collective-permute-start | bytes 1081352 | tf_op jit(solution)/shard_map/ppermute | solution.py:102
  680.8 24.3 %collective-permute-start.63 = (bf16[704,256]{1,0:T(8,128)(2,1)S(1)}, bf16[704,256]{1,0:T(8,128)(2,1)S(1)}, u32[]{:S(2)}, u32[]{:S(2)}) collective-permute-start(bf16[704,256]{1,0:T(8,128)(2,1)S(1)} %constant_dynamic-update-slice_fusion.51), channel_id=1, source_target_pairs={{0,2},{2,0},{4,6},{6,4},{8,10},{10,8},{12,14},{14,12},{16,18},{18,... | collective-permute-start | bytes 1081352 | tf_op jit(solution)/shard_map/ppermute | solution.py:102
  681.9 24.7 %collective-permute-start.107 = (bf16[704,256]{1,0:T(8,128)(2,1)S(1)}, bf16[704,256]{1,0:T(8,128)(2,1)S(1)}, u32[]{:S(2)}, u32[]{:S(2)}) collective-permute-start(bf16[704,256]{1,0:T(8,128)(2,1)S(1)} %constant_dynamic-update-slice_fusion.19), channel_id=1, source_target_pairs={{0,4},{2,6},{4,0},{6,2},{8,12},{10,14},{12,8},{14,10},{16,20},{18,... | collective-permute-start | bytes 1081352 | tf_op jit(solution)/shard_map/ppermute | solution.py:102
  683.1 22.0 %collective-permute-start.73 = (bf16[704,256]{1,0:T(8,128)(2,1)S(1)}, bf16[704,256]{1,0:T(8,128)(2,1)S(1)}, u32[]{:S(2)}, u32[]{:S(2)}) collective-permute-start(bf16[704,256]{1,0:T(8,128)(2,1)S(1)} %constant_dynamic-update-slice_fusion.43), channel_id=1, source_target_pairs={{0,4},{2,6},{4,0},{6,2},{8,12},{10,14},{12,8},{14,10},{16,20},{18,... | collective-permute-start | bytes 1081352 | tf_op jit(solution)/shard_map/ppermute | solution.py:102
  713.3 18.9 %collective-permute-start.122 = (bf16[256,128]{1,0:T(8,128)(2,1)}, bf16[256,128]{1,0:T(8,128)(2,1)}, u32[]{:S(2)}, u32[]{:S(2)}) collective-permute-start(bf16[256,128]{1,0:T(8,128)(2,1)} %reshape.641), channel_id=1, source_target_pairs={{0,1},{1,0},{2,3},{3,2},{4,5},{5,4},{6,7},{7,6},{8,9},{9,8},{10,11... | collective-permute-start | bytes 196616 | tf_op jit(solution)/shard_map/ppermute | solution.py:142
  (253 other events, 3349.1 us)
